TPU v7x, 1024 devices: a whole 8x8x8 slice. The times are simulated.
1024 devices in a mesh: tile: 64 (over z_hi, x, core), band: 8 (over y), chan: 2 (over z_lo).
Axes of the slice: x: 8, y: 8, z: 8 (z_hi: 4, z_lo: 2; z = z_hi * 2 + z_lo), core: 2. Of those that a mesh axis runs over, the one named last changes fastest.
Arguments:
- records: bfloat16 [262144, 128], P(('tile', 'band', 'chan')), may hold values from -6 to 6
- instrument: int32 [262144], P(('tile', 'band', 'chan')), may hold values from 0 to 7
- record_tile: int32 [262144, 1], P(('tile', 'band', 'chan')), may hold values from 0 to 63; in each aligned block of 256 rows (0 to 255, 256 to 511, ...) at most 8 rows name the same one
- record_cell: int32 [262144], P(('tile', 'band', 'chan')), may hold values from 0 to 1023
- inst_gain: float32 [8, 128], replicated, may hold values from 0.5 to 2
- inst_bias: float32 [8, 128], replicated, may hold values from -3 to 3
- embed_weight: bfloat16 [128, 256], P(None, 'chan'), may hold values from -0.5 to 0.5
- dens_weight: float32 [256], P('chan'), may hold values from -5 to 5
- embed_bias: float32 [256], P('chan'), may hold values from -3 to 3
- conv_weight: bfloat16 [2, 3, 3, 256, 256], P(None, None, None, None, 'chan'), may hold values from -0.125 to 0.125
- conv_bias: float32 [2, 256], P(None, 'chan'), may hold values from -3 to 3
Outputs:
- band_field: bfloat16 [64, 8, 1024, 256], P('tile', 'band', None, 'chan')
Inputs may be any that keep to these rules, and one draw needn't show every extreme that they name: `record_tile`: among the 256 rows of one device no tile is named by more than 8 records, a bound that some block reaches.
All inputs are finite; a program needn't handle non-finite values.
Results may differ from a plain program's by a relative error of at most 0.0059.
Values may be sent and summed in bfloat16 or wider, within the bound.
A program may use at most 32 MiB of HBM per device.

v0:
```python
import jax
import jax.numpy as jnp
from jax import lax
from jax.sharding import PartitionSpec as P

LAYERS = 2
LAT_DEV = 64
LON_DEV = 16


def extended(cells, sides, width):
    for axis, dim in sides:
        count = lax.axis_size(axis)
        ends = count - 1
        head = lax.slice_in_dim(cells, 0, width, axis=dim)
        tail = lax.slice_in_dim(cells, cells.shape[dim] - width, cells.shape[dim], axis=dim)
        cells = jnp.concatenate(
            [
                lax.ppermute(tail, axis, [(i, (i + 1) % count) for i in range(ends)]),
                cells,
                lax.ppermute(head, axis, [((i + 1) % count, i) for i in range(ends)]),
            ],
            axis=dim,
        )
    return cells


def bin_cells(values, cell_ids, cell_count):
    onehot = jnp.arange(cell_count, dtype=jnp.int32)[:, None] == cell_ids[None, :]
    totals = jnp.dot(onehot.astype(jnp.bfloat16), values, preferred_element_type=jnp.float32)
    tallies = jnp.sum(onehot.astype(jnp.float32), axis=1)
    return (totals, tallies)


def conv_taps(padded, kernel):
    return lax.conv_general_dilated(
        padded[None],
        kernel,
        (1, 1),
        "VALID",
        dimension_numbers=("NHWC", "HWIO", "NHWC"),
        preferred_element_type=jnp.float32,
    )[0]


def local(
    records,
    instrument,
    record_tile,
    record_cell,
    inst_gain,
    inst_bias,
    embed_weight,
    dens_weight,
    embed_bias,
    conv_weight,
    conv_bias,
):
    n_tile = lax.axis_size("tile")
    row_count = records.shape[0]
    rad_width = records.shape[1]
    capacity = 2 * row_count // n_tile
    cell_count = LAT_DEV * LON_DEV
    picker = (
        instrument[:, None] == jnp.arange(inst_gain.shape[0], dtype=jnp.int32)[None, :]
    ).astype(jnp.float32)
    gain_rows = jnp.dot(picker, inst_gain, precision=lax.Precision.HIGHEST)
    bias_rows = jnp.dot(picker, inst_bias, precision=lax.Precision.HIGHEST)
    corrected = (records.astype(jnp.float32) * gain_rows + bias_rows).astype(jnp.bfloat16)
    target_tile = record_tile[:, 0]
    tile_hits = (target_tile[:, None] == jnp.arange(n_tile, dtype=jnp.int32)[None, :]).astype(
        jnp.int32
    )
    order_in = jnp.sum(jnp.cumsum(tile_hits, axis=0) * tile_hits, axis=1) - 1
    slot_index = target_tile * capacity + order_in
    send_rows = (
        jnp.zeros((n_tile * capacity, rad_width), jnp.bfloat16)
        .at[slot_index]
        .set(corrected)
        .reshape(n_tile, capacity, rad_width)
    )
    send_cells = (
        jnp.full((n_tile * capacity,), -1, jnp.int32)
        .at[slot_index]
        .set(record_cell)
        .reshape(n_tile, capacity)
    )
    arrived, arrived_cells = (
        lax.all_to_all(send_rows, "tile", split_axis=0, concat_axis=0, tiled=True),
        lax.all_to_all(send_cells, "tile", split_axis=0, concat_axis=0, tiled=True),
    )
    arrived = arrived.reshape(-1, rad_width)
    arrived_cells = arrived_cells.reshape(-1)
    totals, tallies = bin_cells(arrived, arrived_cells, cell_count)
    totals, tallies = lax.psum((totals, tallies), "chan")
    averaged = (totals / jnp.maximum(tallies, 1.0)[:, None]).astype(jnp.bfloat16)
    density = tallies / (tallies + 1.0)
    grid_state = jnp.dot(averaged, embed_weight, preferred_element_type=jnp.float32)
    grid_state = grid_state + density[:, None] * dens_weight[None, :] + embed_bias[None, :]
    grid_state = grid_state.astype(jnp.bfloat16).reshape(LAT_DEV, LON_DEV, -1)
    for layer_idx in range(LAYERS):
        kernel = conv_weight[layer_idx]
        full_chan = lax.all_gather(grid_state, "chan", axis=2, tiled=True)
        padded = extended(full_chan, (("band", 0), ("tile", 1)), 1)
        summed = conv_taps(padded, kernel)
        grid_state = (
            grid_state.astype(jnp.float32)
            + jax.nn.gelu(summed + conv_bias[layer_idx][None, None, :])
        ).astype(jnp.bfloat16)
    circles = lax.all_to_all(grid_state, "tile", split_axis=0, concat_axis=1, tiled=True)
    return circles[:, None]


def solution(mesh):
    in_specs = (
        P(("tile", "band", "chan"), None),
        P(("tile", "band", "chan")),
        P(("tile", "band", "chan"), None),
        P(("tile", "band", "chan")),
        P(),
        P(),
        P(None, "chan"),
        P("chan"),
        P("chan"),
        P(None, None, None, None, "chan"),
        P(None, "chan"),
    )
    out_specs = P("tile", "band", None, "chan")
    return jax.shard_map(local, mesh=mesh, in_specs=in_specs, out_specs=out_specs, check_vma=False)
```

profile of v0, /device:TPU:1, one launch (start us, length us, event | category | flops | bytes accessed | tf_op | source)
XLA Modules:
  0.0 209.9 jit_solution(7065498638397091581)
XLA Ops:
  6.5 0.7 fusion.60
  7.2 0.6 reduce-window.6
  7.8 0.2 slice_reduce_fusion
  8.1 0.8 fusion.55
  8.9 0.7 compare_select_fusion
  9.5 1.6 scatter_custom_fusion
  11.1 0.7 all_to_all.16
  11.8 22.7 %all-to-all-start = ((s32[64,1,8]{2,1,0:T(1,128)}), s32[64,1,8]{2,1,0:T(1,128)S(1)}, u32[]{:S(2)}, u32[]{:S(2)}) async-start(s32[64,1,8]{2,1,0:T(1,128)} %bitcast.5), calls=%async_computation | async-start | bytes 65536 | tf_op jit(solution)/shard_map/all_to_all | solution.py:90
  34.6 1.1 convolution_multiply_fusion
  35.7 1.0 fusion.25
  36.7 1.8 scatter_custom_fusion.1
  38.5 7.8 %all-to-all-done = s32[64,1,8]{2,1,0:T(1,128)S(1)} async-done(((s32[64,1,8]{2,1,0:T(1,128)}), s32[64,1,8]{2,1,0:T(1,128)S(1)}, u32[]{:S(2)}, u32[]{:S(2)}) %all-to-all-start) | async-done | bytes 2080 | tf_op jit(solution)/shard_map/all_to_all | solution.py:90
  46.2 5.0 %all-to-all-start.1 = ((bf16[64,8,128]{2,1,0:T(8,128)(2,1)}), bf16[64,8,128]{2,1,0:T(8,128)(2,1)S(1)}, u32[]{:S(2)}, u32[]{:S(2)}) async-start(bf16[64,8,128]{2,1,0:T(8,128)(2,1)} %bitcast.6), calls=%async_computation.1 | async-start | bytes 262144 | tf_op jit(solution)/shard_map/all_to_all | solution.py:89
  51.3 0.6 broadcast.116
  51.9 0.8 reduce.5
  52.7 11.3 %all-to-all-done.1 = bf16[64,8,128]{2,1,0:T(8,128)(2,1)S(1)} async-done(((bf16[64,8,128]{2,1,0:T(8,128)(2,1)}), bf16[64,8,128]{2,1,0:T(8,128)(2,1)S(1)}, u32[]{:S(2)}, u32[]{:S(2)}) %all-to-all-start.1) | async-done | bytes 131104 | tf_op jit(solution)/shard_map/all_to_all | solution.py:89
  64.0 1.3 fusion.2
  65.3 0.3 convert_reduce_fusion
  65.6 4.4 %psum.15 = f32[1024]{0:T(1024)S(1)} all-reduce(f32[1024]{0:T(1024)S(1)} %convert_reduce_fusion), channel_id=1, replica_groups=mesh['tile'=64,'band'=8,'chan'=2] {'chan'}, use_global_device_ids=true, to_apply=%region_7.8 | all-reduce | flops 1024 | bytes 8192 | tf_op jit(solution)/shard_map/psum | solution.py:95
  70.0 41.8 %all-reduce.2.cloned.1.call-done = f32[1024,128]{1,0:T(8,128)} async-done(((f32[1024,128]{1,0:T(8,128)}), f32[1024,128]{1,0:T(8,128)}) %all-reduce.2.cloned.1.call-update) | async-done | bytes 524304 | tf_op jit(solution)/shard_map/psum | solution.py:95
  111.8 1.4 fusion.24
  113.3 7.9 %all_gather.6 = bf16[64,16,256]{2,0,1:T(8,128)(2,1)S(1)} all-gather(bf16[64,16,128]{2,0,1:T(8,128)(2,1)S(1)} %copy.44), channel_id=1, replica_groups=mesh['tile'=64,'band'=8,'chan'=2] {'chan'}, dimensions={2}, use_global_device_ids=true | all-gather | bytes 786432 | tf_op jit(solution)/shard_map/all_gather | solution.py:103
  121.3 3.1 %collective-permute-start = (bf16[1,16,256]{2,0,1:T(2,128)(2,1)S(1)}, bf16[1,16,256]{2,0,1:T(2,128)(2,1)S(1)}, u32[]{:S(2)}, u32[]{:S(2)}) collective-permute-start(bf16[1,16,256]{2,0,1:T(2,128)(2,1)S(1)} %get-tuple-element.11), channel_id=1, source_target_pairs={{0,2},{2,4},{4,6},{6,8},{8,10},{10,12},{12,14},{1,3},{3,5},{5,7},{... | collective-permute-start | bytes 24584 | tf_op jit(solution)/shard_map/ppermute | solution.py:19
  124.4 1.3 collective-permute-start.1
  125.7 3.2 %collective-permute-done.1 = bf16[1,16,256]{2,0,1:T(2,128)(2,1)S(1)} collective-permute-done((bf16[1,16,256]{2,0,1:T(2,128)(2,1)S(1)}, bf16[1,16,256]{2,0,1:T(2,128)(2,1)S(1)}, u32[]{:S(2)}, u32[]{:S(2)}) %collective-permute-start.1) | collective-permute-done | bytes 8224 | tf_op jit(solution)/shard_map/ppermute | solution.py:21
  128.9 5.9 %collective-permute-start.2 = (bf16[66,1,256]{2,0,1:T(8,128)(2,1)S(1)}, bf16[66,1,256]{2,0,1:T(8,128)(2,1)S(1)}, u32[]{:S(2)}, u32[]{:S(2)}) collective-permute-start(bf16[66,1,256]{2,0,1:T(8,128)(2,1)S(1)} %get-tuple-element.7), channel_id=1, source_target_pairs={{0,16},{16,32},{32,48},{48,64},{64,80},{80,96},{96,112},{112,128},... | collective-permute-start | bytes 101384 | tf_op jit(solution)/shard_map/ppermute | solution.py:19
  134.8 1.9 collective-permute-start.3
  136.8 3.3 %collective-permute-done.3 = bf16[66,1,256]{2,0,1:T(8,128)(2,1)S(1)} collective-permute-done((bf16[66,1,256]{2,0,1:T(8,128)(2,1)S(1)}, bf16[66,1,256]{2,0,1:T(8,128)(2,1)S(1)}, u32[]{:S(2)}, u32[]{:S(2)}) %collective-permute-start.3) | collective-permute-done | bytes 33824 | tf_op jit(solution)/shard_map/ppermute | solution.py:21
  140.1 0.3 maximum_bitcast_fusion
  140.5 0.2 copy.47
  140.8 0.9 copy-done.2
  141.8 2.0 fusion.21
  143.8 0.2 copy.48
  144.0 0.2 fusion.41
  144.2 7.0 %all_gather.7 = bf16[64,16,256]{2,0,1:T(8,128)(2,1)S(1)} all-gather(bf16[64,16,128]{2,0,1:T(8,128)(2,1)S(1)} %fusion.41), channel_id=1, replica_groups=mesh['tile'=64,'band'=8,'chan'=2] {'chan'}, dimensions={2}, use_global_device_ids=true | all-gather | bytes 786432 | tf_op jit(solution)/shard_map/all_gather | solution.py:103
  151.3 3.1 %collective-permute-start.4 = (bf16[1,16,256]{2,0,1:T(2,128)(2,1)S(1)}, bf16[1,16,256]{2,0,1:T(2,128)(2,1)S(1)}, u32[]{:S(2)}, u32[]{:S(2)}) collective-permute-start(bf16[1,16,256]{2,0,1:T(2,128)(2,1)S(1)} %get-tuple-element.9), channel_id=1, source_target_pairs={{0,2},{2,4},{4,6},{6,8},{8,10},{10,12},{12,14},{1,3},{3,5},{5,7},{... | collective-permute-start | bytes 24584 | tf_op jit(solution)/shard_map/ppermute | solution.py:19
  154.4 1.3 collective-permute-start.5
  155.7 3.7 %collective-permute-done.5 = bf16[1,16,256]{2,0,1:T(2,128)(2,1)S(1)} collective-permute-done((bf16[1,16,256]{2,0,1:T(2,128)(2,1)S(1)}, bf16[1,16,256]{2,0,1:T(2,128)(2,1)S(1)}, u32[]{:S(2)}, u32[]{:S(2)}) %collective-permute-start.5) | collective-permute-done | bytes 8224 | tf_op jit(solution)/shard_map/ppermute | solution.py:21
  159.4 5.3 %collective-permute-start.6 = (bf16[66,1,256]{2,0,1:T(8,128)(2,1)S(1)}, bf16[66,1,256]{2,0,1:T(8,128)(2,1)S(1)}, u32[]{:S(2)}, u32[]{:S(2)}) collective-permute-start(bf16[66,1,256]{2,0,1:T(8,128)(2,1)S(1)} %get-tuple-element.5), channel_id=1, source_target_pairs={{0,16},{16,32},{32,48},{48,64},{64,80},{80,96},{96,112},{112,128},... | collective-permute-start | bytes 101384 | tf_op jit(solution)/shard_map/ppermute | solution.py:19
  164.7 2.1 %collective-permute-start.7 = (bf16[66,1,256]{2,0,1:T(8,128)(2,1)S(1)}, bf16[66,1,256]{2,0,1:T(8,128)(2,1)S(1)}, u32[]{:S(2)}, u32[]{:S(2)}) collective-permute-start(bf16[66,1,256]{2,0,1:T(8,128)(2,1)S(1)} %get-tuple-element.6), channel_id=1, source_target_pairs={{16,0},{32,16},{48,32},{64,48},{80,64},{96,80},{112,96},{128,112},... | collective-permute-start | bytes 101384 | tf_op jit(solution)/shard_map/ppermute | solution.py:21
  166.8 3.2 %collective-permute-done.7 = bf16[66,1,256]{2,0,1:T(8,128)(2,1)S(1)} collective-permute-done((bf16[66,1,256]{2,0,1:T(8,128)(2,1)S(1)}, bf16[66,1,256]{2,0,1:T(8,128)(2,1)S(1)}, u32[]{:S(2)}, u32[]{:S(2)}) %collective-permute-start.7) | collective-permute-done | bytes 33824 | tf_op jit(solution)/shard_map/ppermute | solution.py:21
  170.0 0.3 maximum_bitcast_fusion.1
  170.4 0.2 copy.50
  170.7 2.1 fusion.18
  172.9 0.2 fusion.50
  173.1 0.2 copy.52
  173.3 29.0 %all_to_all.23 = bf16[64,16,128]{2,1,0:T(8,128)(2,1)S(1)} all-to-all(bf16[64,16,128]{2,1,0:T(8,128)(2,1)S(1)} %copy.52), channel_id=1, replica_groups=mesh['tile'=64,'band'=8,'chan'=2] {'tile'}, dimensions={0} | all-to-all | bytes 524288 | tf_op jit(solution)/shard_map/all_to_all | solution.py:110
  202.3 0.7 copy.58
  (33 shorter events, 1.0 us)
Async XLA Ops:
  6.5 105.3 %copy-start = (bf16[128,128]{1,0:T(8,128)(2,1)S(1)}, bf16[128,128]{1,0:T(8,128)(2,1)}, u32[]{:S(2)}) copy-start(bf16[128,128]{1,0:T(8,128)(2,1)} %param.17) | copy-start | bytes 98308
  11.8 34.4 %all-to-all-start = ((s32[64,1,8]{2,1,0:T(1,128)}), s32[64,1,8]{2,1,0:T(1,128)S(1)}, u32[]{:S(2)}, u32[]{:S(2)}) async-start(s32[64,1,8]{2,1,0:T(1,128)} %bitcast.5), calls=%async_computation | async-start | bytes 65536 | tf_op jit(solution)/shard_map/all_to_all | solution.py:90
  34.5 77.3 %copy-start.3 = (f32[128]{0:T(128)S(1)}, f32[128]{0:T(128)}, u32[]{:S(2)}) copy-start(f32[128]{0:T(128)} %param.19) | copy-start | bytes 1540
  34.6 77.2 %copy-start.4 = (f32[128]{0:T(128)S(1)}, f32[128]{0:T(128)}, u32[]{:S(2)}) copy-start(f32[128]{0:T(128)} %param.18) | copy-start | bytes 1540
  46.2 17.7 %all-to-all-start.1 = ((bf16[64,8,128]{2,1,0:T(8,128)(2,1)}), bf16[64,8,128]{2,1,0:T(8,128)(2,1)S(1)}, u32[]{:S(2)}, u32[]{:S(2)}) async-start(bf16[64,8,128]{2,1,0:T(8,128)(2,1)} %bitcast.6), calls=%async_computation.1 | async-start | bytes 262144 | tf_op jit(solution)/shard_map/all_to_all | solution.py:89
  51.2 60.6 %all-reduce.2.cloned.1.call-start = ((), (), s32[]{:S(2)}) async-start(), calls=%async_computation.3 | async-start | bytes 1048576 | tf_op jit(solution)/shard_map/psum | solution.py:95
  113.2 23.5 %copy-start.1 = (f32[2,128]{1,0:T(2,128)S(1)}, f32[2,128]{1,0:T(2,128)}, u32[]{:S(2)}) copy-start(f32[2,128]{1,0:T(2,128)} %param.21) | copy-start | bytes 3076
  121.3 4.4 %collective-permute-start = (bf16[1,16,256]{2,0,1:T(2,128)(2,1)S(1)}, bf16[1,16,256]{2,0,1:T(2,128)(2,1)S(1)}, u32[]{:S(2)}, u32[]{:S(2)}) collective-permute-start(bf16[1,16,256]{2,0,1:T(2,128)(2,1)S(1)} %get-tuple-element.11), channel_id=1, source_target_pairs={{0,2},{2,4},{4,6},{6,8},{8,10},{10,12},{12,14},{1,3},{3,5},{5,7},{... | collective-permute-start | bytes 24584 | tf_op jit(solution)/shard_map/ppermute | solution.py:19
  124.4 4.5 %collective-permute-start.1 = (bf16[1,16,256]{2,0,1:T(2,128)(2,1)S(1)}, bf16[1,16,256]{2,0,1:T(2,128)(2,1)S(1)}, u32[]{:S(2)}, u32[]{:S(2)}) collective-permute-start(bf16[1,16,256]{2,0,1:T(2,128)(2,1)S(1)} %get-tuple-element.12), channel_id=1, source_target_pairs={{2,0},{4,2},{6,4},{8,6},{10,8},{12,10},{14,12},{3,1},{5,3},{7,5},{... | collective-permute-start | bytes 24584 | tf_op jit(solution)/shard_map/ppermute | solution.py:21
  128.9 7.8 %collective-permute-start.2 = (bf16[66,1,256]{2,0,1:T(8,128)(2,1)S(1)}, bf16[66,1,256]{2,0,1:T(8,128)(2,1)S(1)}, u32[]{:S(2)}, u32[]{:S(2)}) collective-permute-start(bf16[66,1,256]{2,0,1:T(8,128)(2,1)S(1)} %get-tuple-element.7), channel_id=1, source_target_pairs={{0,16},{16,32},{32,48},{48,64},{64,80},{80,96},{96,112},{112,128},... | collective-permute-start | bytes 101384 | tf_op jit(solution)/shard_map/ppermute | solution.py:19
  134.8 5.3 %collective-permute-start.3 = (bf16[66,1,256]{2,0,1:T(8,128)(2,1)S(1)}, bf16[66,1,256]{2,0,1:T(8,128)(2,1)S(1)}, u32[]{:S(2)}, u32[]{:S(2)}) collective-permute-start(bf16[66,1,256]{2,0,1:T(8,128)(2,1)S(1)} %get-tuple-element.8), channel_id=1, source_target_pairs={{16,0},{32,16},{48,32},{64,48},{80,64},{96,80},{112,96},{128,112},... | collective-permute-start | bytes 101384 | tf_op jit(solution)/shard_map/ppermute | solution.py:21
  140.5 1.3 copy-start.2
  140.5 1.3 copy-start.5
  151.3 4.4 %collective-permute-start.4 = (bf16[1,16,256]{2,0,1:T(2,128)(2,1)S(1)}, bf16[1,16,256]{2,0,1:T(2,128)(2,1)S(1)}, u32[]{:S(2)}, u32[]{:S(2)}) collective-permute-start(bf16[1,16,256]{2,0,1:T(2,128)(2,1)S(1)} %get-tuple-element.9), channel_id=1, source_target_pairs={{0,2},{2,4},{4,6},{6,8},{8,10},{10,12},{12,14},{1,3},{3,5},{5,7},{... | collective-permute-start | bytes 24584 | tf_op jit(solution)/shard_map/ppermute | solution.py:19
  154.4 5.0 %collective-permute-start.5 = (bf16[1,16,256]{2,0,1:T(2,128)(2,1)S(1)}, bf16[1,16,256]{2,0,1:T(2,128)(2,1)S(1)}, u32[]{:S(2)}, u32[]{:S(2)}) collective-permute-start(bf16[1,16,256]{2,0,1:T(2,128)(2,1)S(1)} %get-tuple-element.10), channel_id=1, source_target_pairs={{2,0},{4,2},{6,4},{8,6},{10,8},{12,10},{14,12},{3,1},{5,3},{7,5},{... | collective-permute-start | bytes 24584 | tf_op jit(solution)/shard_map/ppermute | solution.py:21
  159.4 7.4 %collective-permute-start.6 = (bf16[66,1,256]{2,0,1:T(8,128)(2,1)S(1)}, bf16[66,1,256]{2,0,1:T(8,128)(2,1)S(1)}, u32[]{:S(2)}, u32[]{:S(2)}) collective-permute-start(bf16[66,1,256]{2,0,1:T(8,128)(2,1)S(1)} %get-tuple-element.5), channel_id=1, source_target_pairs={{0,16},{16,32},{32,48},{48,64},{64,80},{80,96},{96,112},{112,128},... | collective-permute-start | bytes 101384 | tf_op jit(solution)/shard_map/ppermute | solution.py:19
  164.7 5.3 %collective-permute-start.7 = (bf16[66,1,256]{2,0,1:T(8,128)(2,1)S(1)}, bf16[66,1,256]{2,0,1:T(8,128)(2,1)S(1)}, u32[]{:S(2)}, u32[]{:S(2)}) collective-permute-start(bf16[66,1,256]{2,0,1:T(8,128)(2,1)S(1)} %get-tuple-element.6), channel_id=1, source_target_pairs={{16,0},{32,16},{48,32},{64,48},{80,64},{96,80},{112,96},{128,112},... | collective-permute-start | bytes 101384 | tf_op jit(solution)/shard_map/ppermute | solution.py:21
Sparse Core Ops, SparseCore 0:
  65.4 46.3 all-reduce.1
where the time goes:
time: 212 us; the launch traced here: 210 us
  waiting for transfers between devices  74.1 us (35%)
  starting transfers between devices  51.8 us (24%)
  blocking collectives  48.4 us (23%)
  between operations  13.7 us (6%)
  matrix products  8.84 us (4%)
  local copies, waits for them, and re-layouts  7.91 us (4%)
  other arithmetic  5.04 us (2%)
    psum x1, waiting for transfers between devices, local(): totals, tallies = lax.psum((totals, tallies), 'chan')  41.8 us
    all_to_all x1, blocking collectives, local(): lax.all_to_all(grid_state, 'tile', split_axis=0, concat_axis=1, tiled=True)  29 us
    all_to_all x1, starting transfers between devices, local(): lax.all_to_all(send_cells, 'tile', split_axis=0, concat_axis=0, tiled=True)  22.7 us
    ppermute x4, starting transfers between devices, extended(): lax.ppermute(tail, axis, [(i, (i + 1) % count) for i in range(ends)])  17.4 us
    all_gather x2, blocking collectives, local(): full_chan = lax.all_gather(grid_state, 'chan', axis=2, tiled=True)  15 us
    ppermute x4, waiting for transfers between devices, extended(): lax.ppermute(head, axis, [((i + 1) % count, i) for i in range(ends)])  13.3 us
    all_to_all x1, waiting for transfers between devices, local(): lax.all_to_all(send_rows, 'tile', split_axis=0, concat_axis=0, tiled=True)  11.3 us
    all_to_all x1, waiting for transfers between devices, local(): lax.all_to_all(send_cells, 'tile', split_axis=0, concat_axis=0, tiled=True)  7.76 us
  transfers between devices with their start and end apart: 11, of which 7 were waited for; matrix products, arithmetic and copies ran while one was open for 3% of the time, Pallas kernels for 0%

commit v1 on v0

v1 whole, which is shorter than its diff:
```python
import functools
import math

import jax
import jax.numpy as jnp
from jax import lax
from jax.experimental import pallas as pl
from jax.experimental.pallas import tpu as pltpu
from jax.sharding import PartitionSpec as P

MESH = pl.DeviceIdType.MESH
F32, BF16, I32 = jnp.float32, jnp.bfloat16, jnp.int32
LAT_DEV, LON_DEV = 64, 16
HALF = LAT_DEV // 2
EXT = HALF + 4
EP = 48
CAP = 8
C = 256
SIDE = 2 * EP
MSG = 2 * SIDE + 32
NCELL = EXT * LON_DEV


def mm(a, b):
    return jnp.dot(a, b, preferred_element_type=F32)


def gelu(x):
    inner = math.sqrt(2.0 / math.pi) * (x + 0.044715 * (x * x * x))
    return 0.5 * x * (1.0 + jnp.tanh(inner))


def iotas(rows, cols):
    return lax.broadcasted_iota(I32, (rows, cols), 0), lax.broadcasted_iota(I32, (rows, cols), 1)


def onehot(mask):
    return jnp.where(mask, 1.0, 0.0).astype(BF16)


def thirds(x):
    a = x.astype(BF16).astype(F32)
    b = (x - a).astype(BF16).astype(F32)
    return [a, b, x - a - b]


def kernel(
    n_tile, n_band,
    rec, inst, rtile, rcell, gain, bias, ew, dw, eb, cw, cb,
    out,
    send, send_c, recv, recv_c, wh, ewh, small,
    field, cols, msg, rows, x3, xe, x3g, res,
    halo_sel, ins_sel, col_sel, own_sel,
    s_loc, s_rec, r_rec, s_cell, r_cell, s_cell2, r_cell2,
    s_par, r_par, s_w, r_w, s_w2, r_w2, s_halo, r_halo, s_out, r_out,
):
    t, b, c = lax.axis_index("tile"), lax.axis_index("band"), lax.axis_index("chan")
    oc = 1 - c
    west, east = lax.rem(t + n_tile - 1, n_tile), lax.rem(t + 1, n_tile)
    nb = lax.rem(b + n_band - 1 + 2 * c, n_band)
    core = lax.rem(t, 2)
    sibling = t + 1 - 2 * core
    zside = lax.rem(t + n_tile - 16 + 32 * c, n_tile)
    halo_to = ((west, nb), (t, nb), (east, nb))

    def dev(tt, bb, cc):
        return {"tile": tt, "band": bb, "chan": cc}

    def remote(src, dst, ss, rs, to):
        return pltpu.make_async_remote_copy(
            src_ref=src, dst_ref=dst, send_sem=ss, recv_sem=rs, device_id=to, device_id_type=MESH
        )

    barrier = pltpu.get_barrier_semaphore()

    def greet(tt, bb, cc):
        pl.semaphore_signal(barrier, inc=1, device_id=dev(tt, bb, cc), device_id_type=MESH)

    def greet_band(k, carry):
        d = lax.rem(t + k, n_tile)
        greet(d, b, c)
        greet(d, b, oc)
        return carry

    greet(t, b, oc)
    lax.fori_loop(1, n_tile, greet_band, 0)
    for tt, bb in halo_to:
        greet(tt, bb, oc)

    own_w = pltpu.make_async_copy(cw, wh.at[c], s_loc.at[0])
    own_w.start()

    n_inst = gain.shape[0]
    n_rec = rec.shape[0]
    q, _ = iotas(n_inst, n_rec)
    pick = jnp.where(q == inst[...], 1.0, 0.0)
    pick = jnp.concatenate([pick, pick, pick], axis=0).astype(BF16)
    table = jnp.concatenate(
        [jnp.concatenate(thirds(gain[...]), axis=0), jnp.concatenate(thirds(bias[...]), axis=0)],
        axis=1,
    ).astype(BF16)
    lines = lax.dot_general(pick, table, (((0,), (0,)), ((), ())), preferred_element_type=F32)
    fixed = (rec[...].astype(F32) * lines[:, :128] + lines[:, 128:]).astype(BF16)

    q, _ = iotas(n_tile, n_rec)
    hits = q == rtile[...]
    hits_f = jnp.where(hits, 1.0, 0.0)
    q, n = iotas(n_rec, n_rec)
    rank = jnp.sum(hits_f * mm(hits_f.astype(BF16), onehot(q <= n)), axis=0, keepdims=True) - 1.0
    rank = rank.astype(I32)
    slot = rtile[...] * CAP + rank
    q, _ = iotas(n_tile * CAP, n_rec)
    send[...] = mm(onehot(q == slot), fixed).astype(BF16).reshape(n_tile, CAP, 128)
    q, _ = iotas(128, n_rec)
    place = onehot(q == rank)
    cell = rcell[...]
    dims = (((1,), (1,)), ((), ()))
    high = lax.dot_general((hits_f * (cell // 32 + 16).astype(F32)).astype(BF16), place, dims, preferred_element_type=F32)
    low = lax.dot_general((hits_f * lax.rem(cell, 32).astype(F32)).astype(BF16), place, dims, preferred_element_type=F32)
    send_c[...] = (high * 32.0 + low).reshape(n_tile, 1, 128)

    ewh[c] = ew[...]
    small[c, 0:1] = dw[...]
    small[c, 1:2] = eb[...]
    small[c, 2:4] = cb[...]

    pl.semaphore_wait(barrier, 2 * n_tile - 1 + 3)

    def send_cells(k, carry):
        d = lax.rem(t + k, n_tile)
        remote(send_c.at[d], recv_c.at[c, k], s_cell, r_cell, dev(d, b, c)).start()
        return carry

    def send_rows(k, carry):
        d = lax.rem(t + k, n_tile)
        remote(send.at[d], recv.at[c, k], s_rec, r_rec, dev(d, b, c)).start()
        remote(send.at[d], recv.at[c, k], s_rec, r_rec, dev(d, b, oc)).start()
        return carry

    pltpu.make_async_copy(send_c.at[t], recv_c.at[c, 0], r_cell).start()
    pltpu.make_async_copy(send.at[t], recv.at[c, 0], r_rec).start()
    lax.fori_loop(1, n_tile, send_cells, 0)
    remote(send.at[t], recv.at[c, 0], s_rec, r_rec, dev(t, b, oc)).start()
    lax.fori_loop(1, n_tile, send_rows, 0)

    par = [
        remote(ewh.at[c], ewh.at[c], s_par.at[0], r_par.at[0], dev(t, b, oc)),
        remote(small.at[c], small.at[c], s_par.at[1], r_par.at[1], dev(t, b, oc)),
    ]
    for p in par:
        p.start()
    n_w = cw.shape[1]
    quarter = n_w // 4
    near = [pl.ds(pl.multiple_of((2 * core + s) * quarter, 16), quarter) for s in range(2)]
    half = pl.ds(pl.multiple_of(2 * core * quarter, 16), 2 * quarter)
    parts, shares = [], []
    for layer in range(2):
        for s, to in enumerate((dev(t, b, oc), dev(zside, b, oc))):
            i = 2 * layer + s
            parts.append(remote(cw.at[layer, near[s]], wh.at[c, layer, near[s]], s_w.at[i], r_w.at[i], to))
        shares.append(remote(wh.at[oc, layer, half], wh.at[oc, layer, half], s_w2.at[layer], r_w2.at[layer], dev(sibling, b, c)))
    parts[0].start()
    parts[1].start()

    first = 34 * c
    sent = 2 + 30 * c
    lat_ok = jnp.logical_not(jnp.logical_or(jnp.logical_and(b == 0, c == 0), jnp.logical_and(b == n_band - 1, c == 1)))
    lat_ok = lat_ok.astype(I32)
    west_ok = (t > 0).astype(I32)
    east_ok = (t < n_tile - 1).astype(I32)

    q, n = iotas(MSG, NCELL)
    edge = 16 * q + jnp.where(q < EP, 0, jnp.where(q < 2 * EP, 1 - 16 * EP, jnp.where(q < 3 * EP, 14 - 32 * EP, 15 - 48 * EP)))
    m = q - 2 * SIDE
    side = jnp.where(m >= 16, 1, 0)
    m = m - 16 * side
    col = jnp.where(m >= 2, 1, 0)
    corner = (sent + m - 2 * col) * 16 + 14 * side + col
    corner = jnp.where(m < 4, corner, -1)
    col_sel[...] = onehot(n == jnp.where(q < 2 * SIDE, edge, corner))

    q, n = iotas(2 * SIDE, MSG)
    group = jnp.where(q >= EP, 1, 0) + jnp.where(q >= 2 * EP, 1, 0) + jnp.where(q >= 3 * EP, 1, 0)
    e = q - EP * group
    outer = jnp.logical_and(e >= first, e < first + 2)
    corner = 2 * SIDE + jnp.where(group >= 2, 16, 0) + jnp.where(jnp.logical_or(group == 1, group == 3), 2, 0) + e - first
    ok = jnp.where(group >= 2, east_ok, west_ok) * jnp.where(outer, lat_ok, 1)
    target = jnp.where(outer, corner, q)
    target = jnp.where(jnp.logical_and(ok > 0, e < EXT), target, -1)
    halo_sel[...] = onehot(n == target)

    q, n = iotas(NCELL, SIDE)
    ins_sel[...] = onehot(q == jnp.where(n < EP, 16 * n, 16 * (n - EP) + 15))
    q, n = iotas(SIDE, NCELL)
    own_sel[...] = onehot(n == jnp.where(q < EP, 16 * q, 16 * (q - EP) + 15))

    pltpu.make_async_copy(recv_c.at[c], recv_c.at[c], r_cell).wait()
    forward = remote(recv_c.at[c], recv_c.at[c], s_cell2, r_cell2, dev(t, b, oc))
    forward.start()
    parts[0].wait_recv()
    parts[1].wait_recv()
    shares[0].start()
    parts[2].start()
    parts[3].start()
    forward.wait_recv()
    q, n = iotas(n_tile, n_tile * CAP)
    spread = onehot(jnp.logical_and(n >= q * CAP, n < q * CAP + CAP))
    q, n = iotas(CAP, n_tile * CAP)
    mine = q == lax.rem(n, CAP)
    ids = []
    for s in range(2):
        code = recv_c[s].reshape(n_tile, 128)[:, :128]
        high = jnp.floor(code * (1.0 / 32.0))
        low = code - 32.0 * high
        dims = (((0,), (0,)), ((), ()))
        h = lax.dot_general(high.astype(BF16), spread, dims, preferred_element_type=F32)[:CAP]
        lo = lax.dot_general(low.astype(BF16), spread, dims, preferred_element_type=F32)[:CAP]
        ids.append(jnp.sum(jnp.where(mine, h * 32.0 + lo, 0.0), axis=0, keepdims=True))
    ids = jnp.concatenate(ids, axis=1)
    q, _ = iotas(NCELL, 2 * n_tile * CAP)
    hot = onehot(q == ids.astype(I32) - (512 + 16 * (HALF * c - 2)))

    for p in par:
        p.wait_recv()
    pltpu.make_async_copy(recv, recv, r_rec).wait()

    values = recv[...].reshape(2 * n_tile * CAP, 128)
    sums = mm(hot, jnp.concatenate([values, jnp.ones_like(values)], axis=1))
    count = sums[:, 128:]
    averaged = (sums[:, :128] / jnp.maximum(count, 1.0)).astype(BF16)
    density = count / (count + 1.0)
    weights = jnp.concatenate([ewh[0], ewh[1]], axis=1)
    dens = jnp.concatenate([density * small[s, 0:1] + small[s, 1:2] for s in range(2)], axis=1)
    grid = (mm(averaged, weights) + dens).astype(BF16)
    field[...] = grid.reshape(EXT, LON_DEV, C)
    cols[...] = mm(col_sel[...], grid).astype(BF16)

    halo = [
        remote(field.at[pl.ds(sent, 2)], rows, s_halo.at[0], r_halo.at[0], dev(t, nb, oc)),
        remote(cols.at[pl.ds(0, SIDE)], msg.at[pl.ds(SIDE, SIDE)], s_halo.at[1], r_halo.at[1], dev(west, b, c)),
        remote(cols.at[pl.ds(SIDE, SIDE)], msg.at[pl.ds(0, SIDE)], s_halo.at[2], r_halo.at[2], dev(east, b, c)),
        remote(cols.at[pl.ds(2 * SIDE, 16)], msg.at[pl.ds(2 * SIDE + 16, 16)], s_halo.at[3], r_halo.at[3], dev(west, nb, oc)),
        remote(cols.at[pl.ds(2 * SIDE + 16, 16)], msg.at[pl.ds(2 * SIDE, 16)], s_halo.at[4], r_halo.at[4], dev(east, nb, oc)),
    ]
    for h in halo:
        h.start()
    parts[2].wait_recv()
    parts[3].wait_recv()
    shares[1].start()
    shares[0].wait_recv()
    own_w.wait()
    halo[0].wait()
    field[pl.ds(first, 2)] = (rows[...].astype(F32) * lat_ok.astype(F32)).astype(BF16)
    for h in halo[1:]:
        h.wait()

    def weight(layer, i):
        part = pl.ds(i * 3 * C, 3 * C)
        return jnp.concatenate([wh[0, layer, part], wh[1, layer, part]], axis=1)

    def conv_bias(layer):
        return jnp.concatenate([small[0, 2 + layer : 3 + layer], small[1, 2 + layer : 3 + layer]], axis=1)

    def shifted(flat, insert):
        count = flat.shape[0]
        lon = lax.rem(lax.broadcasted_iota(I32, flat.shape, 0), LON_DEV)
        left = jnp.where(lon == 0, insert, pltpu.roll(flat, 1, 0)).astype(BF16)
        right = jnp.where(lon == LON_DEV - 1, insert, pltpu.roll(flat, count - 1, 0)).astype(BF16)
        return left.reshape(-1, LON_DEV, C), right.reshape(-1, LON_DEV, C)

    edges = mm(halo_sel[...], msg[...])
    edges_b = edges.astype(BF16)
    whole = field[...].reshape(NCELL, C)
    own = mm(own_sel[...], whole).astype(BF16)
    insert = mm(ins_sel[...], edges_b[EP : 3 * EP])
    left, right = shifted(whole.astype(F32), insert)
    x3[:, :, 0:C] = left
    x3[:, :, C : 2 * C] = field[...]
    x3[:, :, 2 * C :] = right
    xe[0:EP, 0:C] = edges_b[0:EP]
    xe[0:EP, C : 2 * C] = edges_b[EP : 2 * EP]
    xe[0:EP, 2 * C :] = own[0:EP]
    xe[EP:, 0:C] = own[EP:]
    xe[EP:, C : 2 * C] = edges_b[2 * EP : 3 * EP]
    xe[EP:, 2 * C :] = edges_b[3 * EP :]

    top_bad = jnp.logical_and(b == 0, c == 0).astype(I32)
    low_bad = jnp.logical_and(b == n_band - 1, c == 1).astype(I32)
    y = [mm(xe[...], weight(0, i)) for i in range(3)]
    y = pltpu.roll(y[0], 1, 0) + y[1] + pltpu.roll(y[2], SIDE - 1, 0) + conv_bias(0)
    q, _ = iotas(SIDE, C)
    e = jnp.where(q >= EP, q - EP, q)
    ok = jnp.where(q >= EP, east_ok, west_ok)
    keep = jnp.logical_and(ok > 0, jnp.logical_and(e >= 1 + top_bad, e <= EXT - 2 - low_bad))
    edge_out = jnp.where(keep, edges[EP : 3 * EP] + gelu(y), 0.0).astype(BF16)

    n_out = EXT - 2
    y = mm(x3[0:n_out].reshape(n_out * LON_DEV, 3 * C), weight(0, 0))
    y = y + mm(x3[1 : n_out + 1].reshape(n_out * LON_DEV, 3 * C), weight(0, 1))
    y = y + mm(x3[2 : n_out + 2].reshape(n_out * LON_DEV, 3 * C), weight(0, 2))
    y = gelu(y + conv_bias(0)) + field[1 : n_out + 1].reshape(n_out * LON_DEV, C).astype(F32)
    q, _ = iotas(n_out * LON_DEV, C)
    keep = jnp.logical_and(q >= LON_DEV * top_bad, q < LON_DEV * (n_out - low_bad))
    y = jnp.where(keep, y, 0.0)
    yb = y.astype(BF16)
    insert = mm(ins_sel[LON_DEV : LON_DEV * (n_out + 1), :], edge_out)
    left, right = shifted(yb.astype(F32), insert)
    x3g[:, :, 0:C] = left
    x3g[:, :, C : 2 * C] = yb.reshape(n_out, LON_DEV, C)
    x3g[:, :, 2 * C :] = right

    shares[1].wait_recv()
    chunk = 8
    n_chunk = HALF // chunk
    here = (t // HALF) == c

    def step(g, carry):
        at = lax.rem(g + t // chunk, n_chunk) * chunk
        y = mm(x3g[pl.ds(at, chunk)].reshape(chunk * LON_DEV, 3 * C), weight(1, 0))
        y = y + mm(x3g[pl.ds(at + 1, chunk)].reshape(chunk * LON_DEV, 3 * C), weight(1, 1))
        y = y + mm(x3g[pl.ds(at + 2, chunk)].reshape(chunk * LON_DEV, 3 * C), weight(1, 2))
        base = x3g[pl.ds(at + 1, chunk), :, C : 2 * C].reshape(chunk * LON_DEV, C).astype(F32)
        y = (gelu(y + conv_bias(1)) + base).astype(BF16)
        for s in range(2):
            res[s, pl.ds(at, chunk)] = y[:, 128 * s : 128 * s + 128].reshape(chunk, LON_DEV, 128)

        def deliver(k, carry):
            r = at + lax.rem(k + t, chunk)
            d = HALF * c + r
            mine = out.at[pl.ds(pl.multiple_of(t * LON_DEV, LON_DEV), LON_DEV)]
            remote(res.at[oc, r], mine, s_out, r_out, dev(d, b, oc)).start()

            @pl.when(d != t)
            def _():
                remote(res.at[c, r], mine, s_out, r_out, dev(d, b, c)).start()

            @pl.when(d == t)
            def _():
                pltpu.make_async_copy(res.at[c, r], mine, r_out).start()

            return carry

        lax.fori_loop(0, chunk, deliver, 0)
        return carry

    lax.fori_loop(0, n_chunk, step, 0)

    def sent_bytes(ref, sem):
        pltpu.make_async_copy(ref, ref, sem).wait()

    sent_bytes(send_c.at[pl.ds(0, n_tile - 1)], s_cell)
    sent_bytes(recv.at[0], s_rec)
    sent_bytes(recv.at[0, pl.ds(0, n_tile - 1)], s_rec)
    forward.wait_send()
    for p in par + parts + shares:
        p.wait_send()
    n_lon = n_tile * LON_DEV
    pl.when(here)(lambda: sent_bytes(out.at[pl.ds(0, n_lon - LON_DEV)], s_out))
    pl.when(jnp.logical_not(here))(lambda: sent_bytes(out, s_out))
    sent_bytes(out, r_out)


def local(n_tile, n_band, records, instrument, record_tile, record_cell, inst_gain, inst_bias, embed_weight, dens_weight, embed_bias, conv_weight, conv_bias):
    n_rec = records.shape[0]
    vmem = pl.BlockSpec(memory_space=pltpu.VMEM)
    hbm = pl.BlockSpec(memory_space=pl.ANY)
    dma, scratch = pltpu.SemaphoreType.DMA, pltpu.VMEM
    taps = 9 * C
    result = pl.pallas_call(
        functools.partial(kernel, n_tile, n_band),
        out_shape=jax.ShapeDtypeStruct((n_tile * LON_DEV, 128), BF16),
        in_specs=[vmem] * 9 + [hbm, vmem],
        out_specs=vmem,
        scratch_shapes=[
            scratch((n_tile, CAP, 128), BF16),
            scratch((n_tile, 1, 128), F32),
            scratch((2, n_tile, CAP, 128), BF16),
            scratch((2, n_tile, 1, 128), F32),
            scratch((2, 2, taps, 128), BF16),
            scratch((2, 128, 128), BF16),
            scratch((2, 8, 128), F32),
            scratch((EXT, LON_DEV, C), BF16),
            scratch((MSG, C), BF16),
            scratch((MSG, C), BF16),
            scratch((2, LON_DEV, C), BF16),
            scratch((EXT, LON_DEV, 3 * C), BF16),
            scratch((SIDE, 3 * C), BF16),
            scratch((EXT - 2, LON_DEV, 3 * C), BF16),
            scratch((2, HALF, LON_DEV, 128), BF16),
            scratch((2 * SIDE, MSG), BF16),
            scratch((NCELL, SIDE), BF16),
            scratch((MSG, NCELL), BF16),
            scratch((SIDE, NCELL), BF16),
            dma((1,)), dma, dma, dma, dma, dma, dma,
            dma((2,)), dma((2,)), dma((4,)), dma((4,)), dma((2,)), dma((2,)), dma((5,)), dma((5,)), dma, dma,
        ],
        compiler_params=pltpu.CompilerParams(
            collective_id=0, has_side_effects=True, vmem_limit_bytes=48 * 1024 * 1024
        ),
        name="encode",
    )(
        records,
        instrument.reshape(1, n_rec),
        record_tile.reshape(1, n_rec),
        record_cell.reshape(1, n_rec),
        inst_gain,
        inst_bias,
        embed_weight,
        dens_weight.reshape(1, -1),
        embed_bias.reshape(1, -1),
        conv_weight.reshape(2, taps, -1),
        conv_bias,
    )
    return result[None, None]


def solution(mesh):
    in_specs = (
        P(("tile", "band", "chan"), None),
        P(("tile", "band", "chan")),
        P(("tile", "band", "chan"), None),
        P(("tile", "band", "chan")),
        P(),
        P(),
        P(None, "chan"),
        P("chan"),
        P("chan"),
        P(None, None, None, None, "chan"),
        P(None, "chan"),
    )
    return jax.shard_map(
        functools.partial(local, mesh.shape["tile"], mesh.shape["band"]),
        mesh=mesh,
        in_specs=in_specs,
        out_specs=P("tile", "band", None, "chan"),
        check_vma=False,
    )
```

time: 212 us -> 68.8 us (0.32)
  waiting for transfers between devices: 74.1 us -> 0 us
  Pallas kernels: 0 us -> 59.4 us
  starting transfers between devices: 51.8 us -> 0 us
  blocking collectives: 48.4 us -> 0 us
  between operations: 13.7 us -> 0.02 us
  matrix products: 8.84 us -> 0 us
  other arithmetic: 5.04 us -> 0 us
    pallas_call x0 -> x1, Pallas kernels: none -> 59.4 us  [local(): pl.pallas_call(functools.partial(kernel, n_tile, n_band), out_shape=jax.S...]
    psum x1 -> x0, waiting for transfers between devices: 41.8 us -> none  [local(): totals, tallies = lax.psum((totals, tallies), 'chan')]
    all_to_all x1 -> x0, blocking collectives: 29 us -> none  [local(): lax.all_to_all(grid_state, 'tile', split_axis=0, concat_axis=1, tiled=True)]
    all_to_all x2 -> x0, starting transfers between devices: 27.7 us -> none  [the longest x1 22.7 us: local(): lax.all_to_all(send_cells, 'tile', split_axis=0, concat_axis=0, tiled=True)]
    ppermute x8 -> x0, starting transfers between devices: 24 us -> none  [the longest x4 17.4 us: extended(): lax.ppermute(tail, axis, [(i, (i + 1) % count) for i in range(ends)])]
    all_to_all x2 -> x0, waiting for transfers between devices: 19 us -> none  [the longest x1 11.3 us: local(): lax.all_to_all(send_rows, 'tile', split_axis=0, concat_axis=0, tiled=True)]
    all_gather x2 -> x0, blocking collectives: 15 us -> none  [local(): full_chan = lax.all_gather(grid_state, 'chan', axis=2, tiled=True)]
    ppermute x8 -> x0, waiting for transfers between devices: 13.3 us -> none  [the longest x4 13.3 us: extended(): lax.ppermute(head, axis, [((i + 1) % count, i) for i in range(ends)])]
  transfers between devices with their start and end apart: 11 -> 0, of which waited for: 7 -> 0; matrix products, arithmetic and copies ran while one was open for 3% -> 0% of each run, Pallas kernels for 0% -> 0%
where the time goes in v1:
time: 68.8 us; the launch traced here: 68.4 us
  Pallas kernels  59.4 us (86%)
  local copies, waits for them, and re-layouts  8.97 us (13%)
    pallas_call x1, Pallas kernels, local(): pl.pallas_call(functools.partial(kernel, n_tile, n_band), out_shape=jax.S...  59.4 us
    unnamed x23, local copies, waits for them, and re-layouts  8.97 us

profile of v1, /device:TPU:1, one launch (start us, length us, event | category | flops | bytes accessed | tf_op | source)
XLA Modules:
  0.0 68.4 jit_solution(3263628596517650470)
XLA Ops:
  0.0 0.0 copy-start
  0.0 1.3 %copy-done = bf16[2,3,3,256,128]{4,3,2,1,0:T(8,128)(2,1)S(1)} copy-done((bf16[2,3,3,256,128]{4,3,2,1,0:T(8,128)(2,1)S(1)}, bf16[2,3,3,256,128]{4,3,2,1,0:T(8,128)(2,1)}, u32[]{:S(2)}) %copy-start) | copy-done | bytes 1179672
  1.3 0.0 copy-start.1
  1.3 0.8 %copy-done.1 = bf16[256,128]{1,0:T(8,128)(2,1)S(1)} copy-done((bf16[256,128]{1,0:T(8,128)(2,1)S(1)}, bf16[256,128]{1,0:T(8,128)(2,1)}, u32[]{:S(2)}) %copy-start.1) | copy-done | bytes 65560
  2.1 0.0 copy-start.2
  2.1 0.8 %copy-done.2 = bf16[128,128]{1,0:T(8,128)(2,1)S(1)} copy-done((bf16[128,128]{1,0:T(8,128)(2,1)S(1)}, bf16[128,128]{1,0:T(8,128)(2,1)}, u32[]{:S(2)}) %copy-start.2) | copy-done | bytes 32792
  2.9 0.0 copy-start.3
  2.9 0.7 %copy-done.3 = f32[8,128]{1,0:T(8,128)S(1)} copy-done((f32[8,128]{1,0:T(8,128)S(1)}, f32[8,128]{1,0:T(8,128)}, u32[]{:S(2)}) %copy-start.3) | copy-done | bytes 4120
  3.6 0.0 copy-start.4
  3.6 0.7 %copy-done.4 = f32[8,128]{1,0:T(8,128)S(1)} copy-done((f32[8,128]{1,0:T(8,128)S(1)}, f32[8,128]{1,0:T(8,128)}, u32[]{:S(2)}) %copy-start.4) | copy-done | bytes 4120
  4.2 0.0 copy-start.5
  4.2 0.7 copy-done.5
  4.9 0.0 copy-start.6
  4.9 0.7 copy-done.6
  5.6 0.0 copy-start.7
  5.6 0.7 copy-done.7
  6.3 0.0 copy-start.8
  6.3 0.7 copy-done.8
  7.0 0.0 copy-start.9
  7.0 0.7 copy-done.9
  7.6 0.0 copy-start.10
  7.6 0.7 copy-done.10
  8.3 59.4 %encode.1 = bf16[1024,128]{1,0:T(8,128)(2,1)S(1)} custom-call(bf16[256,128]{1,0:T(8,128)(2,1)S(1)} %copy-done.1, s32[1,256]{1,0:T(1,128)S(1)} %bitcast.9, s32[1,256]{1,0:T(1,128)S(1)} %bitcast.10, s32[1,256]{1,0:T(1,128)S(1)} %bitcast.11, f32[8,128]{1,0:T(8,128)S(1)} %copy-done.3, f32[8,128]{1,0:T(8,128)S(1)} %copy-done.4, bf16[128,128]{1,0:T(8,128)(2,1)S(1)} %copy-done.2, ...), custom_call_target="tpu_custom_call" | custom-call | tf_op jit(solution)/shard_map/encode/pallas_call | solution.py:369
  67.7 0.7 %copy.13 = bf16[1,1,1024,128]{3,2,1,0:T(8,128)(2,1)} copy(bf16[1,1,1024,128]{3,2,1,0:T(8,128)(2,1)S(1)} %bitcast.8) | data formatting | bytes 524288
Async XLA Ops:
  0.0 1.3 %copy-start = (bf16[2,3,3,256,128]{4,3,2,1,0:T(8,128)(2,1)S(1)}, bf16[2,3,3,256,128]{4,3,2,1,0:T(8,128)(2,1)}, u32[]{:S(2)}) copy-start(bf16[2,3,3,256,128]{4,3,2,1,0:T(8,128)(2,1)} %param.20) | copy-start | bytes 3538948
  1.3 0.8 %copy-start.1 = (bf16[256,128]{1,0:T(8,128)(2,1)S(1)}, bf16[256,128]{1,0:T(8,128)(2,1)}, u32[]{:S(2)}) copy-start(bf16[256,128]{1,0:T(8,128)(2,1)} %rec.1) | copy-start | bytes 196612
  2.1 0.8 %copy-start.2 = (bf16[128,128]{1,0:T(8,128)(2,1)S(1)}, bf16[128,128]{1,0:T(8,128)(2,1)}, u32[]{:S(2)}) copy-start(bf16[128,128]{1,0:T(8,128)(2,1)} %ew.1) | copy-start | bytes 98308
  2.9 0.7 %copy-start.3 = (f32[8,128]{1,0:T(8,128)S(1)}, f32[8,128]{1,0:T(8,128)}, u32[]{:S(2)}) copy-start(f32[8,128]{1,0:T(8,128)} %gain.1) | copy-start | bytes 12292
  3.6 0.7 %copy-start.4 = (f32[8,128]{1,0:T(8,128)S(1)}, f32[8,128]{1,0:T(8,128)}, u32[]{:S(2)}) copy-start(f32[8,128]{1,0:T(8,128)} %bias.1) | copy-start | bytes 12292
  4.2 0.7 copy-start.5
  4.9 0.7 copy-start.6
  5.6 0.7 copy-start.7
  6.3 0.7 copy-start.8
  7.0 0.7 copy-start.9
  7.6 0.7 copy-start.10

commit v2 on v1

--- a/solution.py
+++ b/solution.py
@@ -46,8 +46,9 @@
 
 def kernel(
     n_tile, n_band,
-    rec, inst, rtile, rcell, gain, bias, ew, dw, eb, cw, cb,
+    rec_in, inst_in, rtile_in, rcell_in, gain_in, bias_in, ew_in, dw_in, eb_in, cw, cb_in,
     out,
+    rec, inst, rtile, rcell, gain, bias, dw, eb, cb,
     send, send_c, recv, recv_c, wh, ewh, small,
     field, cols, msg, rows, x3, xe, x3g, res,
     halo_sel, ins_sel, col_sel, own_sel,
@@ -71,24 +72,52 @@
             src_ref=src, dst_ref=dst, send_sem=ss, recv_sem=rs, device_id=to, device_id_type=MESH
         )
 
+    taken = [
+        pltpu.make_async_copy(src, dst, s_loc.at[i])
+        for i, (src, dst) in enumerate(
+            [
+                (rtile_in, rtile), (rcell_in, rcell), (inst_in, inst), (gain_in, gain), (bias_in, bias), (rec_in, rec),
+                (dw_in, dw), (eb_in, eb), (cb_in, cb), (ew_in, ewh.at[c]), (cw, wh.at[c]),
+            ]
+        )
+    ]
+    for copy in taken:
+        copy.start()
+    own_w = taken[-1]
+
     barrier = pltpu.get_barrier_semaphore()
 
     def greet(tt, bb, cc):
         pl.semaphore_signal(barrier, inc=1, device_id=dev(tt, bb, cc), device_id_type=MESH)
 
+    plane = 16
+    z_at, in_plane = t // plane, lax.rem(t, plane)
+    x_at = in_plane // 2
+
+    def far_first(k):
+        j, dc = k // 2, lax.rem(k, 2)
+        turn, j = j // 8, lax.rem(j, 8)
+        n_z = n_tile // plane
+        dz = lax.rem(n_z // 2 + (1 - 2 * lax.rem(turn, 2)) * ((turn + 1) // 2) + n_z, n_z)
+        dx = lax.rem(4 + (1 - 2 * lax.rem(j, 2)) * ((j + 1) // 2) + 8, 8)
+        dc = 1 - dc
+        d = lax.rem(z_at + dz, n_z) * plane + lax.rem(x_at + dx, 8) * 2 + lax.rem(core + dc, 2)
+        return d, (dz * 8 + dx) * 2 + dc
+
     def greet_band(k, carry):
-        d = lax.rem(t + k, n_tile)
+        d, _ = far_first(k)
         greet(d, b, c)
         greet(d, b, oc)
         return carry
 
-    greet(t, b, oc)
-    lax.fori_loop(1, n_tile, greet_band, 0)
+    lax.fori_loop(0, n_tile - 1, greet_band, 0)
     for tt, bb in halo_to:
         greet(tt, bb, oc)
-
-    own_w = pltpu.make_async_copy(cw, wh.at[c], s_loc.at[0])
-    own_w.start()
+    greet(t, b, oc)
+
+
+    for copy in taken[:-1]:
+        copy.wait()
 
     n_inst = gain.shape[0]
     n_rec = rec.shape[0]
@@ -119,29 +148,28 @@
     low = lax.dot_general((hits_f * lax.rem(cell, 32).astype(F32)).astype(BF16), place, dims, preferred_element_type=F32)
     send_c[...] = (high * 32.0 + low).reshape(n_tile, 1, 128)
 
-    ewh[c] = ew[...]
     small[c, 0:1] = dw[...]
     small[c, 1:2] = eb[...]
     small[c, 2:4] = cb[...]
 
     pl.semaphore_wait(barrier, 2 * n_tile - 1 + 3)
 
-    def send_cells(k, carry):
-        d = lax.rem(t + k, n_tile)
+    def send_cells(i, carry):
+        d, k = far_first(i)
         remote(send_c.at[d], recv_c.at[c, k], s_cell, r_cell, dev(d, b, c)).start()
         return carry
 
-    def send_rows(k, carry):
-        d = lax.rem(t + k, n_tile)
+    def send_rows(i, carry):
+        d, k = far_first(i)
         remote(send.at[d], recv.at[c, k], s_rec, r_rec, dev(d, b, c)).start()
         remote(send.at[d], recv.at[c, k], s_rec, r_rec, dev(d, b, oc)).start()
         return carry
 
     pltpu.make_async_copy(send_c.at[t], recv_c.at[c, 0], r_cell).start()
     pltpu.make_async_copy(send.at[t], recv.at[c, 0], r_rec).start()
-    lax.fori_loop(1, n_tile, send_cells, 0)
+    lax.fori_loop(0, n_tile - 1, send_cells, 0)
+    lax.fori_loop(0, n_tile - 1, send_rows, 0)
     remote(send.at[t], recv.at[c, 0], s_rec, r_rec, dev(t, b, oc)).start()
-    lax.fori_loop(1, n_tile, send_rows, 0)
 
     par = [
         remote(ewh.at[c], ewh.at[c], s_par.at[0], r_par.at[0], dev(t, b, oc)),
@@ -315,7 +343,9 @@
     here = (t // HALF) == c
 
     def step(g, carry):
-        at = lax.rem(g + t // chunk, n_chunk) * chunk
+        far_z = jnp.where(c == 0, jnp.where(z_at == 1, 0, jnp.where(z_at == 3, 1, jnp.where(z_at == 0, 1, 0))), jnp.where(z_at == 3, 0, jnp.where(z_at == 1, 1, jnp.where(z_at == 2, 1, 0))))
+        zz = lax.rem(far_z + g // 2, 2)
+        at = (zz * 2 + lax.rem(x_at // 4 + 1 + g, 2)) * chunk
         y = mm(x3g[pl.ds(at, chunk)].reshape(chunk * LON_DEV, 3 * C), weight(1, 0))
         y = y + mm(x3g[pl.ds(at + 1, chunk)].reshape(chunk * LON_DEV, 3 * C), weight(1, 1))
         y = y + mm(x3g[pl.ds(at + 2, chunk)].reshape(chunk * LON_DEV, 3 * C), weight(1, 2))
@@ -362,16 +392,24 @@
 
 def local(n_tile, n_band, records, instrument, record_tile, record_cell, inst_gain, inst_bias, embed_weight, dens_weight, embed_bias, conv_weight, conv_bias):
     n_rec = records.shape[0]
-    vmem = pl.BlockSpec(memory_space=pltpu.VMEM)
-    hbm = pl.BlockSpec(memory_space=pl.ANY)
+    hbm = pl.BlockSpec(memory_space=pltpu.HBM)
     dma, scratch = pltpu.SemaphoreType.DMA, pltpu.VMEM
     taps = 9 * C
     result = pl.pallas_call(
         functools.partial(kernel, n_tile, n_band),
         out_shape=jax.ShapeDtypeStruct((n_tile * LON_DEV, 128), BF16),
-        in_specs=[vmem] * 9 + [hbm, vmem],
-        out_specs=vmem,
+        in_specs=[hbm] * 11,
+        out_specs=hbm,
         scratch_shapes=[
+            scratch((n_rec, 128), BF16),
+            scratch((1, n_rec), I32),
+            scratch((1, n_rec), I32),
+            scratch((1, n_rec), I32),
+            scratch(inst_gain.shape, F32),
+            scratch(inst_gain.shape, F32),
+            scratch((1, 128), F32),
+            scratch((1, 128), F32),
+            scratch((2, 128), F32),
             scratch((n_tile, CAP, 128), BF16),
             scratch((n_tile, 1, 128), F32),
             scratch((2, n_tile, CAP, 128), BF16),
@@ -391,11 +429,11 @@
             scratch((NCELL, SIDE), BF16),
             scratch((MSG, NCELL), BF16),
             scratch((SIDE, NCELL), BF16),
-            dma((1,)), dma, dma, dma, dma, dma, dma,
+            dma((11,)), dma, dma, dma, dma, dma, dma,
             dma((2,)), dma((2,)), dma((4,)), dma((4,)), dma((2,)), dma((2,)), dma((5,)), dma((5,)), dma, dma,
         ],
         compiler_params=pltpu.CompilerParams(
-            collective_id=0, has_side_effects=True, vmem_limit_bytes=48 * 1024 * 1024
+            collective_id=0, has_side_effects=True, vmem_limit_bytes=62 * 1024 * 1024
         ),
         name="encode",
     )(

time: 68.8 us -> 63.9 us (0.929)
  local copies, waits for them, and re-layouts: 8.97 us -> 1.67 us
  Pallas kernels: 59.4 us -> 62 us
    unnamed x23 -> x1, local copies, waits for them, and re-layouts: 8.97 us -> 1.67 us
    pallas_call x1, Pallas kernels: 59.4 us -> 62 us  [local(): pl.pallas_call(functools.partial(kernel, n_tile, n_band), out_shape=jax.S...]
where the time goes in v2:
time: 63.9 us; the launch traced here: 63.7 us
  Pallas kernels  62 us (97%)
  local copies, waits for them, and re-layouts  1.67 us (3%)
    pallas_call x1, Pallas kernels, local(): pl.pallas_call(functools.partial(kernel, n_tile, n_band), out_shape=jax.S...  62 us
    unnamed x1, local copies, waits for them, and re-layouts  1.67 us

profile of v2, /device:TPU:1, one launch (start us, length us, event | category | flops | bytes accessed | tf_op | source)
XLA Modules:
  0.0 63.7 jit_solution(13001156676896452018)
XLA Ops:
  0.0 62.0 %encode.1 = bf16[1024,128]{1,0:T(8,128)(2,1)} custom-call(bf16[256,128]{1,0:T(8,128)(2,1)} %rec_in.1, s32[1,256]{1,0:T(1,128)} %bitcast.9, s32[1,256]{1,0:T(1,128)} %bitcast.10, s32[1,256]{1,0:T(1,128)} %bitcast.11, f32[8,128]{1,0:T(8,128)} %gain_in.1, f32[8,128]{1,0:T(8,128)} %bias_in.1, bf16[128,128]{1,0:T(8,128)(2,1)} %ew_in.1, f32[1,128]{1,0:T(1,128)} %bitcast.12, ...), custom_call_target="tpu_custom_call" | custom-call | tf_op jit(solution)/shard_map/encode/pallas_call | solution.py:398
  62.0 1.7 %copy.13 = bf16[1,1,1024,128]{3,2,1,0:T(8,128)(2,1)} copy(bf16[1,1,1024,128]{3,2,1,0:T(8,128)(2,1)} %bitcast.8) | data formatting | bytes 524288

commit v3 on v2

--- a/solution.py
+++ b/solution.py
@@ -187,8 +187,8 @@
             i = 2 * layer + s
             parts.append(remote(cw.at[layer, near[s]], wh.at[c, layer, near[s]], s_w.at[i], r_w.at[i], to))
         shares.append(remote(wh.at[oc, layer, half], wh.at[oc, layer, half], s_w2.at[layer], r_w2.at[layer], dev(sibling, b, c)))
-    parts[0].start()
-    parts[1].start()
+    for p in parts:
+        p.start()
 
     first = 34 * c
     sent = 2 + 30 * c
@@ -228,8 +228,6 @@
     parts[0].wait_recv()
     parts[1].wait_recv()
     shares[0].start()
-    parts[2].start()
-    parts[3].start()
     forward.wait_recv()
     q, n = iotas(n_tile, n_tile * CAP)
     spread = onehot(jnp.logical_and(n >= q * CAP, n < q * CAP + CAP))
@@ -251,6 +249,9 @@
     for p in par:
         p.wait_recv()
     pltpu.make_async_copy(recv, recv, r_rec).wait()
+    parts[2].wait_recv()
+    parts[3].wait_recv()
+    shares[1].start()
 
     values = recv[...].reshape(2 * n_tile * CAP, 128)
     sums = mm(hot, jnp.concatenate([values, jnp.ones_like(values)], axis=1))
@@ -272,9 +273,6 @@
     ]
     for h in halo:
         h.start()
-    parts[2].wait_recv()
-    parts[3].wait_recv()
-    shares[1].start()
     shares[0].wait_recv()
     own_w.wait()
     halo[0].wait()
@@ -393,13 +391,30 @@
 def local(n_tile, n_band, records, instrument, record_tile, record_cell, inst_gain, inst_bias, embed_weight, dens_weight, embed_bias, conv_weight, conv_bias):
     n_rec = records.shape[0]
     hbm = pl.BlockSpec(memory_space=pltpu.HBM)
+    vmem = pl.BlockSpec(memory_space=pltpu.VMEM)
     dma, scratch = pltpu.SemaphoreType.DMA, pltpu.VMEM
     taps = 9 * C
+    args = [
+        pltpu.with_memory_space_constraint(x, pltpu.HBM)
+        for x in (
+            records,
+            instrument.reshape(1, n_rec),
+            record_tile.reshape(1, n_rec),
+            record_cell.reshape(1, n_rec),
+            inst_gain,
+            inst_bias,
+            embed_weight,
+            dens_weight.reshape(1, -1),
+            embed_bias.reshape(1, -1),
+            conv_weight.reshape(2, taps, -1),
+            conv_bias,
+        )
+    ]
     result = pl.pallas_call(
         functools.partial(kernel, n_tile, n_band),
         out_shape=jax.ShapeDtypeStruct((n_tile * LON_DEV, 128), BF16),
         in_specs=[hbm] * 11,
-        out_specs=hbm,
+        out_specs=vmem,
         scratch_shapes=[
             scratch((n_rec, 128), BF16),
             scratch((1, n_rec), I32),
@@ -433,22 +448,10 @@
             dma((2,)), dma((2,)), dma((4,)), dma((4,)), dma((2,)), dma((2,)), dma((5,)), dma((5,)), dma, dma,
         ],
         compiler_params=pltpu.CompilerParams(
-            collective_id=0, has_side_effects=True, vmem_limit_bytes=62 * 1024 * 1024
+            collective_id=0, has_side_effects=True, vmem_limit_bytes=48 * 1024 * 1024
         ),
         name="encode",
-    )(
-        records,
-        instrument.reshape(1, n_rec),
-        record_tile.reshape(1, n_rec),
-        record_cell.reshape(1, n_rec),
-        inst_gain,
-        inst_bias,
-        embed_weight,
-        dens_weight.reshape(1, -1),
-        embed_bias.reshape(1, -1),
-        conv_weight.reshape(2, taps, -1),
-        conv_bias,
-    )
+    )(*args)
     return result[None, None]
 
 

time: 63.9 us -> 65.9 us (1.031)
  Pallas kernels: 62 us -> 65.1 us
  local copies, waits for them, and re-layouts: 1.67 us -> 0.71 us
    pallas_call x1, Pallas kernels: 62 us -> 65.1 us  [local(): pl.pallas_call(functools.partial(kernel, n_tile, n_band), out_shape=jax.S...]
    unnamed x1, local copies, waits for them, and re-layouts: 1.67 us -> 0.71 us
where the time goes in v3:
time: 65.9 us; the launch traced here: 65.8 us
  Pallas kernels  65.1 us (99%)
  local copies, waits for them, and re-layouts  0.71 us (1%)
    pallas_call x1, Pallas kernels, local(): pl.pallas_call(functools.partial(kernel, n_tile, n_band), out_shape=jax.S...  65.1 us

profile of v3, /device:TPU:1, one launch (start us, length us, event | category | flops | bytes accessed | tf_op | source)
XLA Modules:
  0.0 65.8 jit_solution(8344119499406129109)
XLA Ops:
  0.0 65.1 %encode.1 = bf16[1024,128]{1,0:T(8,128)(2,1)S(1)} custom-call(bf16[256,128]{1,0:T(8,128)(2,1)} %rec_in.1, s32[1,256]{1,0:T(1,128)} %bitcast.9, s32[1,256]{1,0:T(1,128)} %bitcast.10, s32[1,256]{1,0:T(1,128)} %bitcast.11, f32[8,128]{1,0:T(8,128)} %gain_in.1, f32[8,128]{1,0:T(8,128)} %bias_in.1, bf16[128,128]{1,0:T(8,128)(2,1)} %ew_in.1, f32[1,128]{1,0:T(1,128)} %bitcast.12, ...), custom_call_target="tpu_custom_call" | custom-call | tf_op jit(solution)/shard_map/encode/pallas_call | solution.py:413
  65.1 0.7 %copy.13 = bf16[1,1,1024,128]{3,2,1,0:T(8,128)(2,1)} copy(bf16[1,1,1024,128]{3,2,1,0:T(8,128)(2,1)S(1)} %bitcast.7) | data formatting | bytes 524288

commit v4 on v3

--- a/solution.py
+++ b/solution.py
@@ -94,23 +94,36 @@
     z_at, in_plane = t // plane, lax.rem(t, plane)
     x_at = in_plane // 2
 
-    def far_first(k):
-        j, dc = k // 2, lax.rem(k, 2)
-        turn, j = j // 8, lax.rem(j, 8)
-        n_z = n_tile // plane
-        dz = lax.rem(n_z // 2 + (1 - 2 * lax.rem(turn, 2)) * ((turn + 1) // 2) + n_z, n_z)
-        dx = lax.rem(4 + (1 - 2 * lax.rem(j, 2)) * ((j + 1) // 2) + 8, 8)
-        dc = 1 - dc
-        d = lax.rem(z_at + dz, n_z) * plane + lax.rem(x_at + dx, 8) * 2 + lax.rem(core + dc, 2)
-        return d, (dz * 8 + dx) * 2 + dc
-
-    def greet_band(k, carry):
-        d, _ = far_first(k)
+    n_z = n_tile // plane
+
+    def far_first(act):
+        def pair(dz, base, dx, both=True):
+            x = x_at + dx
+            x = jnp.where(x >= 8, x - 8, x)
+            d = base + 2 * x
+            k = (dz * 8 + dx) * 2
+            act(d + 1 - core, k + 1)
+            if both:
+                act(d + core, k)
+
+        for dz in (2, 1, 3, 0):
+            z = z_at + dz
+            base = jnp.where(z >= n_z, z - n_z, z) * plane
+
+            def step(j, carry, dz=dz, base=base):
+                pair(dz, base, 4 - j)
+                pair(dz, base, 5 + j)
+                return carry
+
+            lax.fori_loop(0, 3, step, 0)
+            pair(dz, base, 1)
+            pair(dz, base, 0, both=dz != 0)
+
+    def greet_band(d, k):
         greet(d, b, c)
         greet(d, b, oc)
-        return carry
-
-    lax.fori_loop(0, n_tile - 1, greet_band, 0)
+
+    far_first(greet_band)
     for tt, bb in halo_to:
         greet(tt, bb, oc)
     greet(t, b, oc)
@@ -154,21 +167,17 @@
 
     pl.semaphore_wait(barrier, 2 * n_tile - 1 + 3)
 
-    def send_cells(i, carry):
-        d, k = far_first(i)
+    def send_cells(d, k):
         remote(send_c.at[d], recv_c.at[c, k], s_cell, r_cell, dev(d, b, c)).start()
-        return carry
-
-    def send_rows(i, carry):
-        d, k = far_first(i)
+
+    def send_rows(d, k):
         remote(send.at[d], recv.at[c, k], s_rec, r_rec, dev(d, b, c)).start()
         remote(send.at[d], recv.at[c, k], s_rec, r_rec, dev(d, b, oc)).start()
-        return carry
 
     pltpu.make_async_copy(send_c.at[t], recv_c.at[c, 0], r_cell).start()
     pltpu.make_async_copy(send.at[t], recv.at[c, 0], r_rec).start()
-    lax.fori_loop(0, n_tile - 1, send_cells, 0)
-    lax.fori_loop(0, n_tile - 1, send_rows, 0)
+    far_first(send_cells)
+    far_first(send_rows)
     remote(send.at[t], recv.at[c, 0], s_rec, r_rec, dev(t, b, oc)).start()
 
     par = [
@@ -187,8 +196,8 @@
             i = 2 * layer + s
             parts.append(remote(cw.at[layer, near[s]], wh.at[c, layer, near[s]], s_w.at[i], r_w.at[i], to))
         shares.append(remote(wh.at[oc, layer, half], wh.at[oc, layer, half], s_w2.at[layer], r_w2.at[layer], dev(sibling, b, c)))
-    for p in parts:
-        p.start()
+    parts[0].start()
+    parts[1].start()
 
     first = 34 * c
     sent = 2 + 30 * c
@@ -249,9 +258,8 @@
     for p in par:
         p.wait_recv()
     pltpu.make_async_copy(recv, recv, r_rec).wait()
-    parts[2].wait_recv()
-    parts[3].wait_recv()
-    shares[1].start()
+    parts[2].start()
+    parts[3].start()
 
     values = recv[...].reshape(2 * n_tile * CAP, 128)
     sums = mm(hot, jnp.concatenate([values, jnp.ones_like(values)], axis=1))
@@ -294,6 +302,9 @@
         right = jnp.where(lon == LON_DEV - 1, insert, pltpu.roll(flat, count - 1, 0)).astype(BF16)
         return left.reshape(-1, LON_DEV, C), right.reshape(-1, LON_DEV, C)
 
+    parts[2].wait_recv()
+    parts[3].wait_recv()
+    shares[1].start()
     edges = mm(halo_sel[...], msg[...])
     edges_b = edges.astype(BF16)
     whole = field[...].reshape(NCELL, C)

time: 65.9 us -> 58.7 us (0.89)
  Pallas kernels: 65.1 us -> 57.8 us
    pallas_call x1, Pallas kernels: 65.1 us -> 57.8 us  [local(): pl.pallas_call(functools.partial(kernel, n_tile, n_band), out_shape=jax.S...]
where the time goes in v4:
time: 58.7 us; the launch traced here: 58.5 us
  Pallas kernels  57.8 us (98%)
  local copies, waits for them, and re-layouts  0.71 us (1%)
    pallas_call x1, Pallas kernels, local(): pl.pallas_call(functools.partial(kernel, n_tile, n_band), out_shape=jax.S...  57.8 us

profile of v4, /device:TPU:1, one launch (start us, length us, event | category | flops | bytes accessed | tf_op | source)
XLA Modules:
  0.0 58.5 jit_solution(6641648872236213723)
XLA Ops:
  0.0 57.8 %encode.1 = bf16[1024,128]{1,0:T(8,128)(2,1)S(1)} custom-call(bf16[256,128]{1,0:T(8,128)(2,1)} %rec_in.1, s32[1,256]{1,0:T(1,128)} %bitcast.9, s32[1,256]{1,0:T(1,128)} %bitcast.10, s32[1,256]{1,0:T(1,128)} %bitcast.11, f32[8,128]{1,0:T(8,128)} %gain_in.1, f32[8,128]{1,0:T(8,128)} %bias_in.1, bf16[128,128]{1,0:T(8,128)(2,1)} %ew_in.1, f32[1,128]{1,0:T(1,128)} %bitcast.12, ...), custom_call_target="tpu_custom_call" | custom-call | tf_op jit(solution)/shard_map/encode/pallas_call | solution.py:424
  57.8 0.7 %copy.13 = bf16[1,1,1024,128]{3,2,1,0:T(8,128)(2,1)} copy(bf16[1,1,1024,128]{3,2,1,0:T(8,128)(2,1)S(1)} %bitcast.7) | data formatting | bytes 524288

commit v5 on v4

--- a/solution.py
+++ b/solution.py
@@ -287,6 +287,9 @@
     field[pl.ds(first, 2)] = (rows[...].astype(F32) * lat_ok.astype(F32)).astype(BF16)
     for h in halo[1:]:
         h.wait()
+    parts[2].wait_recv()
+    parts[3].wait_recv()
+    shares[1].start()
 
     def weight(layer, i):
         part = pl.ds(i * 3 * C, 3 * C)
@@ -302,9 +305,6 @@
         right = jnp.where(lon == LON_DEV - 1, insert, pltpu.roll(flat, count - 1, 0)).astype(BF16)
         return left.reshape(-1, LON_DEV, C), right.reshape(-1, LON_DEV, C)
 
-    parts[2].wait_recv()
-    parts[3].wait_recv()
-    shares[1].start()
     edges = mm(halo_sel[...], msg[...])
     edges_b = edges.astype(BF16)
     whole = field[...].reshape(NCELL, C)
@@ -350,9 +350,11 @@
     chunk = 8
     n_chunk = HALF // chunk
     here = (t // HALF) == c
+    t_low, t_row = lax.rem(t, chunk), lax.rem(t, HALF)
+
+    far_z = jnp.where(c == 0, jnp.where(z_at == 1, 0, jnp.where(z_at == 3, 1, jnp.where(z_at == 0, 1, 0))), jnp.where(z_at == 3, 0, jnp.where(z_at == 1, 1, jnp.where(z_at == 2, 1, 0))))
 
     def step(g, carry):
-        far_z = jnp.where(c == 0, jnp.where(z_at == 1, 0, jnp.where(z_at == 3, 1, jnp.where(z_at == 0, 1, 0))), jnp.where(z_at == 3, 0, jnp.where(z_at == 1, 1, jnp.where(z_at == 2, 1, 0))))
         zz = lax.rem(far_z + g // 2, 2)
         at = (zz * 2 + lax.rem(x_at // 4 + 1 + g, 2)) * chunk
         y = mm(x3g[pl.ds(at, chunk)].reshape(chunk * LON_DEV, 3 * C), weight(1, 0))
@@ -363,23 +365,31 @@
         for s in range(2):
             res[s, pl.ds(at, chunk)] = y[:, 128 * s : 128 * s + 128].reshape(chunk, LON_DEV, 128)
 
-        def deliver(k, carry):
-            r = at + lax.rem(k + t, chunk)
-            d = HALF * c + r
-            mine = out.at[pl.ds(pl.multiple_of(t * LON_DEV, LON_DEV), LON_DEV)]
-            remote(res.at[oc, r], mine, s_out, r_out, dev(d, b, oc)).start()
-
-            @pl.when(d != t)
-            def _():
-                remote(res.at[c, r], mine, s_out, r_out, dev(d, b, c)).start()
-
-            @pl.when(d == t)
-            def _():
-                pltpu.make_async_copy(res.at[c, r], mine, r_out).start()
-
-            return carry
-
-        lax.fori_loop(0, chunk, deliver, 0)
+        mine = out.at[pl.ds(pl.multiple_of(t * LON_DEV, LON_DEV), LON_DEV)]
+
+        def row(k):
+            r = k + t_low
+            return at + jnp.where(r >= chunk, r - chunk, r)
+
+        def deliver(r, cc):
+            remote(res.at[cc, r], mine, s_out, r_out, dev(HALF * c + r, b, cc)).start()
+
+        stays = jnp.logical_and(here, jnp.logical_and(at <= t_row, t_row < at + chunk))
+
+        @pl.when(jnp.logical_not(stays))
+        def _():
+            for k in range(chunk):
+                deliver(row(k), oc)
+                deliver(row(k), c)
+
+        @pl.when(stays)
+        def _():
+            pltpu.make_async_copy(res.at[c, t_row], mine, r_out).start()
+            deliver(row(0), oc)
+            for k in range(1, chunk):
+                deliver(row(k), oc)
+                deliver(row(k), c)
+
         return carry
 
     lax.fori_loop(0, n_chunk, step, 0)

time: 58.7 us -> 58.4 us (level)
  no operation moved by 1% of the time
where the time goes in v5:
time: 58.4 us; the launch traced here: 58.3 us
  Pallas kernels  57.6 us (99%)
  local copies, waits for them, and re-layouts  0.71 us (1%)
    pallas_call x1, Pallas kernels, local(): pl.pallas_call(functools.partial(kernel, n_tile, n_band), out_shape=jax.S...  57.6 us

profile of v5, /device:TPU:1, one launch (start us, length us, event | category | flops | bytes accessed | tf_op | source)
XLA Modules:
  0.0 58.3 jit_solution(9950826734942519645)
XLA Ops:
  0.0 57.6 %encode.1 = bf16[1024,128]{1,0:T(8,128)(2,1)S(1)} custom-call(bf16[256,128]{1,0:T(8,128)(2,1)} %rec_in.1, s32[1,256]{1,0:T(1,128)} %bitcast.9, s32[1,256]{1,0:T(1,128)} %bitcast.10, s32[1,256]{1,0:T(1,128)} %bitcast.11, f32[8,128]{1,0:T(8,128)} %gain_in.1, f32[8,128]{1,0:T(8,128)} %bias_in.1, bf16[128,128]{1,0:T(8,128)(2,1)} %ew_in.1, f32[1,128]{1,0:T(1,128)} %bitcast.12, ...), custom_call_target="tpu_custom_call" | custom-call | tf_op jit(solution)/shard_map/encode/pallas_call | solution.py:434
  57.6 0.7 %copy.13 = bf16[1,1,1024,128]{3,2,1,0:T(8,128)(2,1)} copy(bf16[1,1,1024,128]{3,2,1,0:T(8,128)(2,1)S(1)} %bitcast.7) | data formatting | bytes 524288
